TPU v7x, 512 devices: a whole 4x4x16 slice. The times are simulated.
512 devices in a mesh: blk: 16 (over x_hi, y, core), dom: 32 (over z, x_lo).
Axes of the slice: x: 4 (x_hi: 2, x_lo: 2; x = x_hi * 2 + x_lo), y: 4, z: 16, core: 2. Of those that a mesh axis runs over, the one named last changes fastest.
Arguments:
- features: bfloat16 [32, 8192, 256], P('dom', 'blk'), may hold values from -6 to 6
- weight: bfloat16 [256, 256], replicated, may hold values from -0.375 to 0.375
- tiles: bfloat16 [32, 16, 16, 6, 128, 128], P('dom', 'blk'), may hold values from -0.15234375 to 0.15234375
- tile_pos: int32 [32, 16, 16, 6], P('dom', 'blk'), may hold values from 0 to 15, as said below
- tile_count: int32 [32, 16, 16], P('dom', 'blk'), may hold values from 1 to 6
- send_list: int32 [32, 16, 32, 32], P('dom', 'blk'), may hold values from 0 to 511
- send_count: int32 [32, 16, 32], P('dom', 'blk'), may hold values from 0 to 32, as said below
- owner_map: int32 [32, 16, 32, 32], P('dom', 'blk'), may hold values from 0 to 511
- halo_weight: float32 [32, 16, 32, 32], P('dom', 'blk'), may hold values from 0.25 to 1
- cotangent: bfloat16 [32, 8192, 256], P('dom', 'blk'), may hold values from -6 to 6
Outputs:
- layer_out: bfloat16 [32, 8192, 256], P('dom', 'blk')
- feature_grad: bfloat16 [32, 8192, 256], P('dom', 'blk')
- weight_grad: float32 [256, 256], replicated
Inputs may be any that keep to these rules, and one draw needn't show every extreme that they name: `tile_pos`: the 6 positions of one row group in one column group are distinct. `send_count`: zero where the peer is the sender's own partition.
All inputs are finite; a program needn't handle non-finite values.
Results may differ from a plain program's by a relative error of at most 0.019.
Values may be sent and summed in bfloat16 or wider, within the bound.
A program may use at most 128 MiB of HBM per device.

v0:
```python
import jax
import jax.numpy as jnp
from jax import lax
from jax.sharding import PartitionSpec as P


def spread_rows(tile_set, positions, counts, panel, per):
    groups, slots = positions.shape
    tile = tile_set.shape[-1]
    width = panel.shape[-1]
    grid = panel.reshape(groups, per, tile, width)
    column = positions % per
    row_tile = positions // per
    picked = grid[jnp.arange(groups)[:, None], column]
    product = jnp.einsum("gtij,gtjf->gtif", tile_set, picked, preferred_element_type=jnp.float32)
    live = jnp.arange(slots)[None, :] < counts[:, None]
    select = ((row_tile[..., None] == jnp.arange(per)[None, None, :]) & live[..., None]).astype(
        jnp.float32
    )
    return jnp.einsum("gtif,gtr->rif", product, select).reshape(per * tile, width)


def spread_cols(tile_set, positions, counts, grad_rows, per):
    groups, slots = positions.shape
    tile = tile_set.shape[-1]
    width = grad_rows.shape[-1]
    grid = grad_rows.reshape(per, tile, width)
    column = positions % per
    row_tile = positions // per
    picked = grid[row_tile]
    product = jnp.einsum("gtij,gtif->gtjf", tile_set, picked, preferred_element_type=jnp.float32)
    live = jnp.arange(slots)[None, :] < counts[:, None]
    select = ((column[..., None] == jnp.arange(per)[None, None, :]) & live[..., None]).astype(
        jnp.float32
    )
    return jnp.einsum("gtjf,gtc->gcjf", product, select).reshape(groups * per * tile, width)


def on_device(
    features,
    weight,
    tiles,
    tile_pos,
    tile_count,
    send_list,
    send_count,
    owner_map,
    halo_weight,
    cotangent,
):
    feats = features[0]
    rows, width = feats.shape
    tile_set = tiles[0, 0]
    positions = tile_pos[0, 0]
    counts = tile_count[0, 0]
    tile = tile_set.shape[-1]
    per = rows // tile
    send_rows = send_list[0, 0]
    send_live = send_count[0, 0]
    owners = owner_map[0, 0]
    edge_weight = halo_weight[0, 0]
    grad_in = cotangent[0]
    slots = send_rows.shape[1]
    live = (jnp.arange(slots)[None, :] < send_live[:, None])[..., None]
    empty = jnp.zeros((rows, width), jnp.float32)
    projected = jnp.dot(feats, weight, preferred_element_type=jnp.float32).astype(jnp.bfloat16)
    part_tiles = tile_set
    part_pos = positions
    part_count = counts
    local = spread_rows(
        part_tiles, part_pos, part_count, lax.all_gather(projected, "blk", axis=0, tiled=True), per
    )
    outgoing = jnp.where(live, projected[send_rows], jnp.zeros((), jnp.bfloat16))
    incoming = lax.all_to_all(outgoing, "dom", split_axis=0, concat_axis=0, tiled=True)
    weighted = edge_weight.reshape(-1, 1) * incoming.reshape(-1, width).astype(jnp.float32)
    halo_sum = empty.at[owners.reshape(-1)].add(weighted)
    layer_out = (local + halo_sum).astype(jnp.bfloat16)
    back = (edge_weight[..., None] * grad_in[owners].astype(jnp.float32)).astype(jnp.bfloat16)
    returned = lax.all_to_all(back, "dom", split_axis=0, concat_axis=0, tiled=True)
    returned = jnp.where(live, returned, jnp.zeros((), jnp.bfloat16))
    halo_back = empty.at[send_rows.reshape(-1)].add(returned.reshape(-1, width).astype(jnp.float32))
    part_tiles = tile_set
    part_pos = positions
    part_count = counts
    local_grad = lax.psum_scatter(
        spread_cols(part_tiles, part_pos, part_count, grad_in, per).astype(jnp.bfloat16),
        "blk",
        scatter_dimension=0,
        tiled=True,
    ).astype(jnp.float32)
    proj_grad = (local_grad + halo_back).astype(jnp.bfloat16)
    feature_grad = lax.dot_general(
        proj_grad, weight, (((1,), (1,)), ((), ())), preferred_element_type=jnp.float32
    )
    feature_grad = feature_grad.astype(jnp.bfloat16)
    weight_term = lax.dot_general(
        feats, proj_grad, (((0,), (0,)), ((), ())), preferred_element_type=jnp.float32
    )
    total = lax.psum(weight_term, ("blk", "dom"))
    scale = float(lax.axis_size("blk") * lax.axis_size("dom") * rows) ** (-0.5)
    return (layer_out[None], feature_grad[None], total * scale)


def solution(mesh):
    return jax.shard_map(
        on_device,
        mesh=mesh,
        in_specs=(
            P("dom", "blk", None),
            P(),
            P("dom", "blk", None, None, None, None),
            P("dom", "blk", None, None),
            P("dom", "blk", None),
            P("dom", "blk", None, None),
            P("dom", "blk", None),
            P("dom", "blk", None, None),
            P("dom", "blk", None, None),
            P("dom", "blk", None),
        ),
        out_specs=(P("dom", "blk", None), P("dom", "blk", None), P()),
        check_vma=False,
    )
```

profile of v0, /device:TPU:1, one launch (start us, length us, event | category | flops | bytes accessed | tf_op | source)
XLA Modules:
  0.0 745.6 jit_solution(18372749111417586942)
XLA Ops:
  7.2 1.4 compare_select_fusion.4
  8.7 1.3 add_select_fusion
  10.0 0.1 copy.24
  10.0 0.1 reshape.340
  10.1 6.9 gather_fusion.2
  17.0 7.3 fusion.7
  24.3 11.7 %copy.29 = bf16[16,6,256,128]{2,1,3,0:T(8,128)(2,1)} copy(bf16[16,6,256,128]{3,2,1,0:T(8,128)(2,1)} %fusion.7) | data formatting | bytes 12582912 | tf_op jit(solution)/shard_map/gtij,gtif->gtjf/dot_general | solution.py:31
  36.0 0.1 copy.23
  36.2 5.7 fusion.4
  41.9 2.8 copy.25
  44.7 0.6 compare_select_fusion
  45.4 0.8 reshape.348
  46.2 5.0 gather_fusion.3
  51.1 2.0 fusion.17
  53.2 17.1 %all-to-all-start.1 = ((bf16[32,32,256]{2,1,0:T(8,128)(2,1)}), bf16[32,32,256]{2,1,0:T(8,128)(2,1)}, u32[]{:S(2)}, u32[]{:S(2)}) async-start(bf16[32,32,256]{2,1,0:T(8,128)(2,1)} %fusion.17), calls=%async_computation.2 | async-start | bytes 1048576 | tf_op jit(solution)/shard_map/all_to_all | solution.py:79
  70.4 0.8 reshape_squeeze.12
  71.2 0.7 compare_select_fusion.1
  71.9 0.1 reshape.332
  72.0 1.2 convolution_convert_fusion.1
  73.2 5.0 gather_fusion.1
  78.2 0.7 iota_compare_fusion.2
  78.9 0.6 compare_select_fusion.2
  79.5 21.9 %all-to-all-done.1 = bf16[32,32,256]{2,1,0:T(8,128)(2,1)} async-done(((bf16[32,32,256]{2,1,0:T(8,128)(2,1)}), bf16[32,32,256]{2,1,0:T(8,128)(2,1)}, u32[]{:S(2)}, u32[]{:S(2)}) %all-to-all-start.1) | async-done | bytes 524320 | tf_op jit(solution)/shard_map/all_to_all | solution.py:79
  101.4 2.4 broadcast_select_fusion
  103.7 48.7 %reduce-scatter.2.cloned.1.call-done = bf16[512,256]{1,0:T(8,128)(2,1)} async-done(((bf16[8192,256]{1,0:T(8,128)(2,1)}), bf16[512,256]{1,0:T(8,128)(2,1)}) %reduce-scatter.2.cloned.1.call-update) | async-done | bytes 262160 | tf_op jit(solution)/shard_map/reduce_scatter | solution.py:85
  152.4 1.8 convert_element_type.47
  154.2 8.3 %scatter_custom_fusion.1 = f32[512,256]{1,0:T(8,128)} fusion(f32[512,256]{1,0:T(8,128)} %convert_element_type.47, s32[1024]{0:T(1024)} %bitcast.130, bf16[1024,256]{1,0:T(8,128)(2,1)} %bitcast.127), kind=kCustom, calls=%fused_computation.20 | custom fusion | flops 524288 | bytes 1048576 | tf_op jit(solution)/shard_map/scatter-add | solution.py:81
  162.5 2.1 convolution_bitcast_fusion
  164.7 0.7 all-gather.2.cloned.1.call-update
  165.3 0.8 reshape_squeeze.10
  166.1 0.8 mul.26
  166.9 12.4 %all-to-all-start = ((bf16[32,32,256]{2,1,0:T(8,128)(2,1)}), bf16[32,32,256]{2,1,0:T(8,128)(2,1)}, u32[]{:S(2)}, u32[]{:S(2)}) async-start(bf16[32,32,256]{2,1,0:T(8,128)(2,1)} %get-tuple-element.12), calls=%async_computation | async-start | bytes 1048576 | tf_op jit(solution)/shard_map/all_to_all | solution.py:74
  179.4 0.1 copy.20
  179.5 0.1 reshape.324
  179.6 0.1 copy.19
  179.7 0.1 copy.21
  179.8 2.0 fusion.14
  181.8 444.9 %all-reduce.2.cloned.1.call-done = f32[256,256]{0,1:T(8,128)} async-done(((f32[256,256]{0,1:T(8,128)}), f32[256,256]{0,1:T(8,128)}) %all-reduce.2.cloned.1.call-update) | async-done | bytes 262160 | tf_op jit(solution)/shard_map/psum | solution.py:99
  626.7 1.0 broadcast_multiply_fusion
  627.7 0.8 copy.26
  628.5 70.2 %all-gather.2.cloned.1.call-done = bf16[8192,256]{1,0:T(8,128)(2,1)} async-done(((bf16[512,256]{1,0:T(8,128)(2,1)}), bf16[8192,256]{1,0:T(8,128)(2,1)}) %all-gather.2.cloned.1.call-update) | async-done | bytes 4194320 | tf_op jit(solution)/shard_map/all_gather | solution.py:71
  698.8 8.8 %gather_fusion = bf16[96,128,256]{2,1,0:T(8,128)(2,1)} fusion(bf16[16,4,128,256]{3,2,1,0:T(8,128)(2,1)} %bitcast.123, s32[96]{0:T(128)S(1)} %reshape.324), kind=kCustom, calls=%fused_computation | custom fusion | bytes 12583680 | tf_op jit(solution)/shard_map/gather | solution.py:14
  707.6 7.3 fusion.9
  714.8 9.1 %copy.27 = bf16[16,6,256,128]{2,0,1,3:T(8,128)(2,1)} copy(bf16[16,6,256,128]{3,2,1,0:T(8,128)(2,1)} %fusion.9) | data formatting | bytes 12582912 | tf_op jit(solution)/shard_map/gtij,gtjf->gtif/dot_general | solution.py:15
  723.9 3.8 fusion.11
  727.7 0.9 copy.22
  728.6 8.7 %scatter_custom_fusion = f32[512,256]{1,0:T(8,128)} fusion(f32[512,256]{1,0:T(8,128)} %bitcast.126, s32[1024]{0:T(1024)S(1)} %bitcast.129, bf16[1024,256]{1,0:T(8,128)(2,1)} %bitcast.31, f32[1024]{0:T(1024)S(1)} %mul.26), kind=kCustom, calls=%fused_computation.25 | custom fusion | flops 786432 | bytes 1052672 | tf_op jit(solution)/shard_map/scatter-add | solution.py:76
  737.3 1.8 convert_bitcast_fusion
  (33 shorter events, 0.3 us)
Async XLA Ops:
  7.2 9.8 %copy-start = (bf16[1,1,16,6,128,128]{5,4,3,2,1,0:T(8,128)(2,1)S(1)}, bf16[1,1,16,6,128,128]{5,4,3,2,1,0:T(8,128)(2,1)}, u32[]{:S(2)}) copy-start(bf16[1,1,16,6,128,128]{5,4,3,2,1,0:T(8,128)(2,1)} %param.12) | copy-start | bytes 9437188
  7.2 145.2 %reduce-scatter.2.cloned.1.call-start = ((), (), s32[]{:S(2)}) async-start(), calls=%async_computation.4 | async-start | bytes 4456448 | tf_op jit(solution)/shard_map/reduce_scatter | solution.py:85
  24.3 11.8 %copy-start.9 = (s32[1,1,16]{2,1,0:T(1,128)S(1)}, s32[1,1,16]{2,1,0:T(1,128)}, u32[]{:S(2)}) copy-start(s32[1,1,16]{2,1,0:T(1,128)} %param.14) | copy-start | bytes 196
  36.2 5.7 copy-start.5
  41.9 2.8 copy-start.4
  41.9 4.2 copy-start.1
  44.7 27.3 %copy-start.3 = (bf16[256,256]{1,0:T(8,128)(2,1)S(1)}, bf16[256,256]{1,0:T(8,128)(2,1)}, u32[]{:S(2)}) copy-start(bf16[256,256]{1,0:T(8,128)(2,1)} %param.11) | copy-start | bytes 393220
  53.2 48.2 %all-to-all-start.1 = ((bf16[32,32,256]{2,1,0:T(8,128)(2,1)}), bf16[32,32,256]{2,1,0:T(8,128)(2,1)}, u32[]{:S(2)}, u32[]{:S(2)}) async-start(bf16[32,32,256]{2,1,0:T(8,128)(2,1)} %fusion.17), calls=%async_computation.2 | async-start | bytes 1048576 | tf_op jit(solution)/shard_map/all_to_all | solution.py:79
  70.3 109.3 %copy-start.7 = (s32[16,6]{0,1:T(8,128)S(1)}, s32[16,6]{0,1:T(8,128)}, u32[]{:S(2)}) copy-start(s32[16,6]{0,1:T(8,128)} %get-tuple-element.14) | copy-start | bytes 1156
  70.3 109.4 %copy-start.6 = (pred[16,6]{1,0:T(8,128)(4,1)S(1)}, pred[16,6]{1,0:T(8,128)(4,1)}, u32[]{:S(2)}) copy-start(pred[16,6]{1,0:T(8,128)(4,1)} %copy-done.5) | copy-start | bytes 292
  70.3 556.4 %all-reduce.2.cloned.1.call-start = ((), (), s32[]{:S(2)}) async-start(), calls=%async_computation.5 | async-start | bytes 524288 | tf_op jit(solution)/shard_map/psum | solution.py:99
  73.2 91.5 %copy-start.2 = (bf16[512,256]{1,0:T(8,128)(2,1)}, bf16[512,256]{1,0:T(8,128)(2,1)S(1)}, u32[]{:S(2)}) copy-start(bf16[512,256]{1,0:T(8,128)(2,1)S(1)} %convolution_convert_fusion.1) | copy-start | bytes 786436
  79.5 99.9 %copy-start.8 = (s32[16,6,1]{0,2,1:T(1,128)S(1)}, s32[16,6,1]{0,2,1:T(1,128)}, u32[]{:S(2)}) copy-start(s32[16,6,1]{0,2,1:T(1,128)} %get-tuple-element.10) | copy-start | bytes 1156
  164.6 534.2 %all-gather.2.cloned.1.call-start = ((), (), s32[]{:S(2)}) async-start(), calls=%async_computation.3 | async-start | bytes 4456448 | tf_op jit(solution)/shard_map/all_gather | solution.py:71
  166.9 561.7 %all-to-all-start = ((bf16[32,32,256]{2,1,0:T(8,128)(2,1)}), bf16[32,32,256]{2,1,0:T(8,128)(2,1)}, u32[]{:S(2)}, u32[]{:S(2)}) async-start(bf16[32,32,256]{2,1,0:T(8,128)(2,1)} %get-tuple-element.12), calls=%async_computation | async-start | bytes 1048576 | tf_op jit(solution)/shard_map/all_to_all | solution.py:74
Sparse Core Ops, SparseCore 0:
  44.9 107.5 reduce-scatter.1
  164.7 461.9 all-reduce.1
  630.6 68.0 all-gather.1
where the time goes:
time: 747 us; the launch traced here: 746 us
  waiting for transfers between devices  586 us (78%)
  local copies, waits for them, and re-layouts  54.8 us (7%)
  other arithmetic  31.5 us (4%)
  starting transfers between devices  29.7 us (4%)
  matrix products  29.4 us (4%)
  between operations  13.9 us (2%)
    psum x1, waiting for transfers between devices, on_device(): total = lax.psum(weight_term, ('blk', 'dom'))  445 us
    all_gather x1, waiting for transfers between devices, on_device(): lax.all_gather(projected, 'blk', axis=0, tiled=True)  70.2 us
    reduce_scatter x1, waiting for transfers between devices, on_device(): lax.psum_scatter(spread_cols(part_tiles, part_pos, part_count, grad_in, p...  48.7 us
    all_to_all x1, waiting for transfers between devices, on_device(): lax.all_to_all(back, 'dom', split_axis=0, concat_axis=0, tiled=True)  21.9 us
    all_to_all x1, starting transfers between devices, on_device(): lax.all_to_all(back, 'dom', split_axis=0, concat_axis=0, tiled=True)  17.1 us
  transfers between devices with their start and end apart: 5, of which 4 were waited for; matrix products, arithmetic and copies ran while one was open for 7% of the time, Pallas kernels for 0%

commit v1 on v0

--- a/solution.py
+++ b/solution.py
@@ -96,7 +96,7 @@
     weight_term = lax.dot_general(
         feats, proj_grad, (((0,), (0,)), ((), ())), preferred_element_type=jnp.float32
     )
-    total = lax.psum(weight_term, ("blk", "dom"))
+    total = lax.psum(lax.psum(weight_term, "dom"), "blk")
     scale = float(lax.axis_size("blk") * lax.axis_size("dom") * rows) ** (-0.5)
     return (layer_out[None], feature_grad[None], total * scale)
 

time: 747 us -> 707 us (0.946)
  waiting for transfers between devices: 586 us -> 549 us
    psum x1 -> x2, waiting for transfers between devices: 445 us -> 403 us  [on_device(): total = lax.psum(lax.psum(weight_term, 'dom'), 'blk')]
  transfers between devices with their start and end apart: 5 -> 6, of which waited for: 4 -> 5; matrix products, arithmetic and copies ran while one was open for 7% -> 8% of each run, Pallas kernels for 0% -> 0%
where the time goes in v1:
time: 707 us; the launch traced here: 705 us
  waiting for transfers between devices  549 us (78%)
  local copies, waits for them, and re-layouts  54.8 us (8%)
  other arithmetic  31.5 us (4%)
  matrix products  29.4 us (4%)
  starting transfers between devices  26.3 us (4%)
  between operations  13.9 us (2%)
    psum x2, waiting for transfers between devices, on_device(): total = lax.psum(lax.psum(weight_term, 'dom'), 'blk')  403 us
    all_gather x1, waiting for transfers between devices, on_device(): lax.all_gather(projected, 'blk', axis=0, tiled=True)  74.7 us
    reduce_scatter x1, waiting for transfers between devices, on_device(): lax.psum_scatter(spread_cols(part_tiles, part_pos, part_count, grad_in, p...  48.7 us
    all_to_all x1, waiting for transfers between devices, on_device(): lax.all_to_all(back, 'dom', split_axis=0, concat_axis=0, tiled=True)  21.9 us
    all_to_all x1, starting transfers between devices, on_device(): lax.all_to_all(back, 'dom', split_axis=0, concat_axis=0, tiled=True)  17.1 us
  transfers between devices with their start and end apart: 6, of which 5 were waited for; matrix products, arithmetic and copies ran while one was open for 8% of the time, Pallas kernels for 0%

profile of v1, /device:TPU:1, one launch (start us, length us, event | category | flops | bytes accessed | tf_op | source)
XLA Modules:
  0.0 705.1 jit_solution(15689746616510293321)
XLA Ops:
  7.2 1.4 compare_select_fusion.4
  8.7 1.3 add_select_fusion
  10.0 0.1 copy.24
  10.0 0.1 reshape.340
  10.1 6.9 gather_fusion.2
  17.0 7.3 %fusion.7 = bf16[16,6,256,128]{3,2,1,0:T(8,128)(2,1)} fusion(bf16[16,6,128,256]{3,2,1,0:T(8,128)(2,1)} %bitcast.121, bf16[1,1,16,6,128,128]{5,4,3,2,1,0:T(8,128)(2,1)S(1)} %copy-done), kind=kOutput, calls=%fused_computation.11 | convolution fusion | flops 805306368 | bytes 15728640 | tf_op jit(solution)/shard_map/gtij,gtif->gtjf/dot_general | solution.py:31
  24.3 11.7 %copy.29 = bf16[16,6,256,128]{2,1,3,0:T(8,128)(2,1)} copy(bf16[16,6,256,128]{3,2,1,0:T(8,128)(2,1)} %fusion.7) | data formatting | bytes 12582912 | tf_op jit(solution)/shard_map/gtij,gtif->gtjf/dot_general | solution.py:31
  36.0 0.1 copy.23
  36.2 5.7 fusion.4
  41.9 2.8 copy.25
  44.7 0.6 compare_select_fusion
  45.4 0.8 reshape.348
  46.2 5.0 gather_fusion.3
  51.1 2.0 fusion.17
  53.2 17.1 %all-to-all-start.1 = ((bf16[32,32,256]{2,1,0:T(8,128)(2,1)}), bf16[32,32,256]{2,1,0:T(8,128)(2,1)}, u32[]{:S(2)}, u32[]{:S(2)}) async-start(bf16[32,32,256]{2,1,0:T(8,128)(2,1)} %fusion.17), calls=%async_computation.2 | async-start | bytes 1048576 | tf_op jit(solution)/shard_map/all_to_all | solution.py:79
  70.4 0.8 reshape_squeeze.12
  71.2 0.7 compare_select_fusion.1
  72.0 1.2 convolution_convert_fusion.1
  73.2 5.0 gather_fusion.1
  78.2 0.7 iota_compare_fusion.2
  78.9 0.6 compare_select_fusion.2
  79.5 21.9 %all-to-all-done.1 = bf16[32,32,256]{2,1,0:T(8,128)(2,1)} async-done(((bf16[32,32,256]{2,1,0:T(8,128)(2,1)}), bf16[32,32,256]{2,1,0:T(8,128)(2,1)}, u32[]{:S(2)}, u32[]{:S(2)}) %all-to-all-start.1) | async-done | bytes 524320 | tf_op jit(solution)/shard_map/all_to_all | solution.py:79
  101.4 2.4 broadcast_select_fusion
  103.7 48.7 %reduce-scatter.2.cloned.1.call-done = bf16[512,256]{1,0:T(8,128)(2,1)} async-done(((bf16[8192,256]{1,0:T(8,128)(2,1)}), bf16[512,256]{1,0:T(8,128)(2,1)}) %reduce-scatter.2.cloned.1.call-update) | async-done | bytes 262160 | tf_op jit(solution)/shard_map/reduce_scatter | solution.py:85
  152.4 1.8 convert_element_type.47
  154.2 8.3 %scatter_custom_fusion.1 = f32[512,256]{1,0:T(8,128)} fusion(f32[512,256]{1,0:T(8,128)} %convert_element_type.47, s32[1024]{0:T(1024)} %bitcast.130, bf16[1024,256]{1,0:T(8,128)(2,1)} %bitcast.127), kind=kCustom, calls=%fused_computation.20 | custom fusion | flops 524288 | bytes 1048576 | tf_op jit(solution)/shard_map/scatter-add | solution.py:81
  162.5 2.1 convolution_bitcast_fusion
  164.6 241.2 %all-reduce.3.cloned.1.call-done = f32[256,256]{0,1:T(8,128)} async-done(((f32[256,256]{0,1:T(8,128)}), f32[256,256]{0,1:T(8,128)}) %all-reduce.3.cloned.1.call-update) | async-done | bytes 262160 | tf_op jit(solution)/shard_map/psum | solution.py:99
  406.0 0.5 all-gather.2.cloned.1.call-update
  406.5 0.8 reshape_squeeze.10
  407.3 0.8 mul.26
  408.1 9.0 %all-to-all-start = ((bf16[32,32,256]{2,1,0:T(8,128)(2,1)}), bf16[32,32,256]{2,1,0:T(8,128)(2,1)}, u32[]{:S(2)}, u32[]{:S(2)}) async-start(bf16[32,32,256]{2,1,0:T(8,128)(2,1)} %get-tuple-element.12), calls=%async_computation | async-start | bytes 1048576 | tf_op jit(solution)/shard_map/all_to_all | solution.py:74
  417.1 0.1 copy.20
  417.2 0.1 reshape.324
  417.3 0.1 copy.19
  417.4 0.1 copy.21
  417.5 2.0 fusion.14
  419.5 162.2 %all-reduce.5.cloned.1.call-done = f32[256,256]{0,1:T(8,128)} async-done(((f32[256,256]{0,1:T(8,128)}), f32[256,256]{0,1:T(8,128)}) %all-reduce.5.cloned.1.call-update) | async-done | bytes 262160 | tf_op jit(solution)/shard_map/psum | solution.py:99
  581.7 1.0 broadcast_multiply_fusion
  582.7 0.8 copy.26
  583.5 74.7 %all-gather.2.cloned.1.call-done = bf16[8192,256]{1,0:T(8,128)(2,1)} async-done(((bf16[512,256]{1,0:T(8,128)(2,1)}), bf16[8192,256]{1,0:T(8,128)(2,1)}) %all-gather.2.cloned.1.call-update) | async-done | bytes 4194320 | tf_op jit(solution)/shard_map/all_gather | solution.py:71
  658.2 8.8 %gather_fusion = bf16[96,128,256]{2,1,0:T(8,128)(2,1)} fusion(bf16[16,4,128,256]{3,2,1,0:T(8,128)(2,1)} %bitcast.123, s32[96]{0:T(128)S(1)} %reshape.324), kind=kCustom, calls=%fused_computation | custom fusion | bytes 12583680 | tf_op jit(solution)/shard_map/gather | solution.py:14
  667.0 7.3 %fusion.9 = bf16[16,6,256,128]{3,2,1,0:T(8,128)(2,1)} fusion(bf16[16,6,128,256]{3,2,1,0:T(8,128)(2,1)} %bitcast.120, bf16[1,1,16,6,128,128]{5,4,3,2,1,0:T(8,128)(2,1)S(1)} %copy-done), kind=kOutput, calls=%fused_computation.13 | convolution fusion | flops 805306368 | bytes 15728640 | tf_op jit(solution)/shard_map/gtij,gtjf->gtif/dot_general | solution.py:15
  674.3 9.1 %copy.27 = bf16[16,6,256,128]{2,0,1,3:T(8,128)(2,1)} copy(bf16[16,6,256,128]{3,2,1,0:T(8,128)(2,1)} %fusion.9) | data formatting | bytes 12582912 | tf_op jit(solution)/shard_map/gtij,gtjf->gtif/dot_general | solution.py:15
  683.4 3.8 fusion.11
  687.2 0.9 copy.22
  688.1 8.7 %scatter_custom_fusion = f32[512,256]{1,0:T(8,128)} fusion(f32[512,256]{1,0:T(8,128)} %bitcast.126, s32[1024]{0:T(1024)S(1)} %bitcast.129, bf16[1024,256]{1,0:T(8,128)(2,1)} %bitcast.31, f32[1024]{0:T(1024)S(1)} %mul.26), kind=kCustom, calls=%fused_computation.25 | custom fusion | flops 786432 | bytes 1052672 | tf_op jit(solution)/shard_map/scatter-add | solution.py:76
  696.8 1.8 convert_bitcast_fusion
  (36 shorter events, 0.5 us)
Async XLA Ops:
  7.2 9.8 %copy-start = (bf16[1,1,16,6,128,128]{5,4,3,2,1,0:T(8,128)(2,1)S(1)}, bf16[1,1,16,6,128,128]{5,4,3,2,1,0:T(8,128)(2,1)}, u32[]{:S(2)}) copy-start(bf16[1,1,16,6,128,128]{5,4,3,2,1,0:T(8,128)(2,1)} %param.12) | copy-start | bytes 9437188
  7.2 145.2 %reduce-scatter.2.cloned.1.call-start = ((), (), s32[]{:S(2)}) async-start(), calls=%async_computation.4 | async-start | bytes 4456448 | tf_op jit(solution)/shard_map/reduce_scatter | solution.py:85
  24.3 11.8 %copy-start.9 = (s32[1,1,16]{2,1,0:T(1,128)S(1)}, s32[1,1,16]{2,1,0:T(1,128)}, u32[]{:S(2)}) copy-start(s32[1,1,16]{2,1,0:T(1,128)} %param.14) | copy-start | bytes 196
  36.2 5.7 copy-start.5
  41.9 2.8 copy-start.4
  41.9 4.2 copy-start.1
  44.7 27.3 %copy-start.3 = (bf16[256,256]{1,0:T(8,128)(2,1)S(1)}, bf16[256,256]{1,0:T(8,128)(2,1)}, u32[]{:S(2)}) copy-start(bf16[256,256]{1,0:T(8,128)(2,1)} %param.11) | copy-start | bytes 393220
  53.2 48.2 %all-to-all-start.1 = ((bf16[32,32,256]{2,1,0:T(8,128)(2,1)}), bf16[32,32,256]{2,1,0:T(8,128)(2,1)}, u32[]{:S(2)}, u32[]{:S(2)}) async-start(bf16[32,32,256]{2,1,0:T(8,128)(2,1)} %fusion.17), calls=%async_computation.2 | async-start | bytes 1048576 | tf_op jit(solution)/shard_map/all_to_all | solution.py:79
  70.3 347.0 %copy-start.7 = (s32[16,6]{0,1:T(8,128)S(1)}, s32[16,6]{0,1:T(8,128)}, u32[]{:S(2)}) copy-start(s32[16,6]{0,1:T(8,128)} %get-tuple-element.14) | copy-start | bytes 1156
  70.3 347.1 %copy-start.6 = (pred[16,6]{1,0:T(8,128)(4,1)S(1)}, pred[16,6]{1,0:T(8,128)(4,1)}, u32[]{:S(2)}) copy-start(pred[16,6]{1,0:T(8,128)(4,1)} %copy-done.5) | copy-start | bytes 292
  70.3 335.6 %all-reduce.3.cloned.1.call-start = ((), (), s32[]{:S(2)}) async-start(), calls=%async_computation.5 | async-start | bytes 524288 | tf_op jit(solution)/shard_map/psum | solution.py:99
  73.2 332.8 %copy-start.2 = (bf16[512,256]{1,0:T(8,128)(2,1)}, bf16[512,256]{1,0:T(8,128)(2,1)S(1)}, u32[]{:S(2)}) copy-start(bf16[512,256]{1,0:T(8,128)(2,1)S(1)} %convolution_convert_fusion.1) | copy-start | bytes 786436
  79.5 337.6 %copy-start.8 = (s32[16,6,1]{0,2,1:T(1,128)S(1)}, s32[16,6,1]{0,2,1:T(1,128)}, u32[]{:S(2)}) copy-start(s32[16,6,1]{0,2,1:T(1,128)} %get-tuple-element.10) | copy-start | bytes 1156
  164.6 417.1 %all-reduce.5.cloned.1.call-start = ((), (), s32[]{:S(2)}) async-start(), calls=%async_computation.6 | async-start | bytes 524288 | tf_op jit(solution)/shard_map/psum | solution.py:99
  405.9 252.3 %all-gather.2.cloned.1.call-start = ((), (), s32[]{:S(2)}) async-start(), calls=%async_computation.3 | async-start | bytes 4456448 | tf_op jit(solution)/shard_map/all_gather | solution.py:71
  408.1 280.0 %all-to-all-start = ((bf16[32,32,256]{2,1,0:T(8,128)(2,1)}), bf16[32,32,256]{2,1,0:T(8,128)(2,1)}, u32[]{:S(2)}, u32[]{:S(2)}) async-start(bf16[32,32,256]{2,1,0:T(8,128)(2,1)} %get-tuple-element.12), calls=%async_computation | async-start | bytes 1048576 | tf_op jit(solution)/shard_map/all_to_all | solution.py:74
Sparse Core Ops, SparseCore 0:
  44.9 107.5 reduce-scatter.1
  164.7 241.1 all-reduce.2
  408.8 172.8 all-reduce.4
  586.0 72.1 all-gather.1
